TPU v7x, 512 devices: a whole 4x4x16 slice. The times are simulated.
512 devices in a mesh: lon: 128 (over x, z, y_lo), lat: 4 (over y_hi, core).
Axes of the slice: x: 4, y: 4 (y_hi: 2, y_lo: 2; y = y_hi * 2 + y_lo), z: 16, core: 2. Of those that a mesh axis runs over, the one named last changes fastest.
Arguments:
- features: bfloat16 [512, 1024, 256], P('lat', 'lon'), may hold values from -2048 to 2048
- cotangent: bfloat16 [512, 1024, 256], P('lat', 'lon'), may hold values from -96 to 96
- kernel: bfloat16 [3, 3, 256, 256], replicated, may hold values from -0.125 to 0.125
- norm_gain: float32 [256], replicated, may hold values from 0.25 to 1.75
- norm_shift: float32 [256], replicated, may hold values from -3 to 3
Outputs:
- feature_grad: bfloat16 [512, 1024, 256], P('lat', 'lon')
- kernel_grad: float32 [3, 3, 256, 256], replicated
- gain_grad: float32 [256], replicated
- shift_grad: float32 [256], replicated
All inputs are finite; a program needn't handle non-finite values.
Results may differ from a plain program's by a relative error of at most 0.0024.
Values may be sent and summed in bfloat16 or wider, within the bound.
A program may use at most 64 MiB of HBM per device.

v0:
```python
import jax
import jax.numpy as jnp
from jax import lax
from jax.sharding import PartitionSpec as P

GROUPS = 32


norm_eps = 1e-06


def with_halo(cells, sides, width, closed):
    for axis, dim in sides:
        count = lax.axis_size(axis)
        ends = count if closed else count - 1
        head = lax.slice_in_dim(cells, 0, width, axis=dim)
        tail = lax.slice_in_dim(cells, cells.shape[dim] - width, cells.shape[dim], axis=dim)
        cells = jnp.concatenate(
            [
                lax.ppermute(tail, axis, [(i, (i + 1) % count) for i in range(ends)]),
                cells,
                lax.ppermute(head, axis, [((i + 1) % count, i) for i in range(ends)]),
            ],
            axis=dim,
        )
    return cells


def passed_along(value, axis, steps):
    count = lax.axis_size(axis)
    pairs = [(source, (source + steps) % count) for source in range(count)]
    return lax.ppermute(value, axis, pairs)


def group_total(per_channel, groups):
    return jnp.sum(per_channel.reshape(groups, -1), axis=1)


def local(features, cotangent, kernel, norm_gain, norm_shift):
    lat_rows, lon_cols, channels = features.shape
    group_size = channels // GROUPS
    lon_count = lax.axis_size("lon")
    lat_count = lax.axis_size("lat")
    cell_count = float(lat_rows * lon_cols * lon_count * lat_count)
    group_cells = cell_count * group_size
    values = features.astype(jnp.float32)
    channel_sum = jnp.sum(values, axis=(0, 1))
    group_mean = lax.psum(group_total(channel_sum, GROUPS), ("lon", "lat")) / group_cells
    mean_full = jnp.repeat(group_mean, group_size)
    centered = values - mean_full
    spread = group_total(jnp.sum(centered * centered, axis=(0, 1)), GROUPS)
    group_var = lax.psum(spread, ("lon", "lat")) / group_cells
    inverse_std = jnp.repeat(1.0 / jnp.sqrt(group_var + norm_eps), group_size)
    standard_part = (features.astype(jnp.float32) - mean_full) * inverse_std
    normed = standard_part * norm_gain + norm_shift
    lat_index = lax.axis_index("lat")
    at_top = lat_index == 0
    at_bottom = lat_index == lat_count - 1
    half_turn = lon_count // 2
    hidden = jax.nn.silu(normed).astype(jnp.bfloat16)
    wide_hidden = with_halo(hidden, (("lon", 1),), 1, True)
    full_hidden = with_halo(wide_hidden, (("lat", 0),), 1, False)
    pole_hidden = passed_along(jnp.stack([wide_hidden[0], wide_hidden[-1]]), "lon", half_turn)
    wide_cot = with_halo(cotangent, (("lon", 1),), 1, True)
    full_cot = with_halo(wide_cot, (("lat", 0),), 1, False)
    pole_cot = passed_along(jnp.stack([wide_cot[0], wide_cot[-1]]), "lon", half_turn)
    upper_row = jnp.where(at_top, pole_hidden[0], full_hidden[0])
    lower_row = jnp.where(at_bottom, pole_hidden[1], full_hidden[-1])
    padded = jnp.concatenate([upper_row[None], full_hidden[1:-1], lower_row[None]], axis=0)
    windows = [
        padded[tap_row : tap_row + lat_rows, tap_col : tap_col + lon_cols]
        for tap_row in range(3)
        for tap_col in range(3)
    ]
    patches = jnp.concatenate(windows, axis=2).reshape(-1, 9 * channels)
    flat_cot = cotangent.reshape(-1, channels)
    local_kernel = lax.dot_general(
        patches, flat_cot, (((0,), (0,)), ((), ())), preferred_element_type=jnp.float32
    ).reshape(3, 3, channels, channels)
    flipped = jnp.transpose(kernel, (0, 1, 3, 2))
    cot_windows = [
        full_cot[2 - tap_row : 2 - tap_row + lat_rows, 2 - tap_col : 2 - tap_col + lon_cols]
        for tap_row in range(3)
        for tap_col in range(3)
    ]
    cot_patches = jnp.concatenate(cot_windows, axis=2).reshape(-1, 9 * channels)
    hidden_grad = jnp.dot(
        cot_patches, flipped.reshape(9 * channels, channels), preferred_element_type=jnp.float32
    ).reshape(lat_rows, lon_cols, channels)

    def pole_term(wrapped, tap_row):
        strip = jnp.concatenate(
            [wrapped[2 - tap_col : 2 - tap_col + lon_cols] for tap_col in range(3)], axis=1
        )
        return jnp.dot(
            strip,
            flipped[tap_row].reshape(3 * channels, channels),
            preferred_element_type=jnp.float32,
        )

    hidden_grad = hidden_grad.at[0].add(jnp.where(at_top, pole_term(pole_cot[0], 0), 0.0))
    hidden_grad = hidden_grad.at[lat_rows - 1].add(
        jnp.where(at_bottom, pole_term(pole_cot[1], 2), 0.0)
    )
    logistic = jax.nn.sigmoid(normed)
    normed_grad = hidden_grad * logistic * (1.0 + normed * (1.0 - logistic))
    first_sum, second_sum = lax.psum(
        (jnp.sum(normed_grad, axis=(0, 1)), jnp.sum(normed_grad * standard_part, axis=(0, 1))),
        ("lon", "lat"),
    )
    shift_grad = first_sum / cell_count
    gain_grad = second_sum / cell_count
    first_mean = jnp.repeat(group_total(norm_gain * shift_grad, GROUPS) / group_size, group_size)
    second_mean = jnp.repeat(group_total(norm_gain * gain_grad, GROUPS) / group_size, group_size)
    feature_grad = (
        inverse_std * (normed_grad * norm_gain - first_mean - standard_part * second_mean)
    ).astype(jnp.bfloat16)
    kernel_total = lax.psum(local_kernel, ("lon", "lat"))
    kernel_grad = kernel_total / cell_count
    return (feature_grad, kernel_grad, gain_grad, shift_grad)


def solution(mesh):
    placed = (P("lat", "lon", None), P("lat", "lon", None), P(), P(), P())
    return jax.shard_map(
        local,
        mesh=mesh,
        in_specs=placed,
        out_specs=(P("lat", "lon", None), P(), P(), P()),
        check_vma=False,
    )
```

profile of v0, /device:TPU:1, one launch (start us, length us, event | category | flops | bytes accessed | tf_op | source)
XLA Modules:
  0.0 773.8 jit_solution(15492471137930510179)
XLA Ops:
  7.2 1.3 convert_reduce_fusion
  8.6 1.2 copy.52
  9.8 4.0 collective-permute-start
  13.9 109.9 %psum.35 = f32[32]{0:T(128)S(1)} all-reduce(f32[32]{0:T(128)S(1)} %reduce_sum.73), channel_id=1, replica_groups=mesh['lon'=128,'lat'=4] {'lon','lat'}, use_global_device_ids=true, to_apply=%region_2.0 | all-reduce | flops 32 | bytes 256 | tf_op jit(solution)/shard_map/psum | solution.py:48
  123.9 1.3 fusion.21
  125.4 3.5 collective-permute-start.1
  129.0 98.6 %psum.36 = f32[32]{0:T(128)S(1)} all-reduce(f32[32]{0:T(128)S(1)} %reduce_sum.75), channel_id=1, replica_groups=mesh['lon'=128,'lat'=4] {'lon','lat'}, use_global_device_ids=true, to_apply=%region_5.0 | all-reduce | flops 32 | bytes 256 | tf_op jit(solution)/shard_map/psum | solution.py:52
  227.5 1.6 copy.58
  229.5 2.6 collective-permute-start.2
  232.1 4.5 collective-permute-start.3
  236.7 3.1 collective-permute-start.4
  240.9 1.4 fusion.59
  242.8 0.4 copy-done.2
  243.2 1.5 scatter-add.6
  244.9 0.9 slice_add_fusion
  245.8 1.5 scatter-add.9
  247.3 1.9 fusion.50
  249.2 4.2 collective-permute-start.6
  253.4 1.9 collective-permute-start.5
  255.4 7.9 %collective-permute-done.5 = bf16[128,1,256]{2,0,1:T(8,128)(2,1)S(1)} collective-permute-done((bf16[128,1,256]{2,0,1:T(8,128)(2,1)S(1)}, bf16[128,1,256]{2,0,1:T(8,128)(2,1)S(1)}, u32[]{:S(2)}, u32[]{:S(2)}) %collective-permute-start.5) | collective-permute-done | bytes 65568 | tf_op jit(solution)/shard_map/ppermute | solution.py:20
  263.4 1.9 collective-permute-start.7
  265.3 2.3 collective-permute-start.9
  267.6 4.9 collective-permute-start.8
  272.6 0.6 collective-permute-done.8
  274.1 4.7 copy.89
  278.8 6.7 copy.62
  285.5 5.1 fusion.36
  290.7 100.6 %all-reduce = (f32[256]{0:T(256)S(1)}, f32[256]{0:T(256)S(1)}) all-reduce(f32[256]{0:T(256)S(1)} %get-tuple-element.45, f32[256]{0:T(256)S(1)} %get-tuple-element.44), channel_id=1, replica_groups=mesh['lon'=128,'lat'=4] {'lon','lat'}, use_global_device_ids=true, to_apply=%region_10.11 | all-reduce | flops 512 | bytes 4096 | tf_op jit(solution)/shard_map/psum | solution.py:107
  391.3 0.6 fusion.51
  393.0 1.1 copy.63
  394.0 369.7 %all-reduce.3.cloned.1.call-done = f32[3,3,256,256]{3,2,1,0:T(8,128)} async-done(((f32[3,3,256,256]{3,2,1,0:T(8,128)}), f32[3,3,256,256]{3,2,1,0:T(8,128)}) %all-reduce.3.cloned.1.call-update) | async-done | bytes 2359312 | tf_op jit(solution)/shard_map/psum | solution.py:118
  763.7 3.3 broadcast_multiply_fusion
  (79 shorter events, 4.7 us)
Async XLA Ops:
  7.2 222.2 %copy-start.1 = (bf16[128,8,256]{2,1,0:T(8,128)(2,1)S(1)}, bf16[128,8,256]{2,1,0:T(8,128)(2,1)}, u32[]{:S(2)}) copy-start(bf16[128,8,256]{2,1,0:T(8,128)(2,1)} %param.10) | copy-start | bytes 1572868
  7.2 756.5 %all-reduce.3.cloned.1.call-start = ((), (), s32[]{:S(2)}) async-start(), calls=%async_computation | async-start | bytes 4718592 | tf_op jit(solution)/shard_map/psum | solution.py:118
  9.8 219.5 %collective-permute-start = (bf16[128,1,256]{2,0,1:T(8,128)(2,1)S(1)}, bf16[128,1,256]{2,0,1:T(8,128)(2,1)S(1)}, u32[]{:S(2)}, u32[]{:S(2)}) collective-permute-start(bf16[128,1,256]{2,0,1:T(8,128)(2,1)S(1)} %get-tuple-element.65), channel_id=1, source_target_pairs={{0,4},{4,8},{8,12},{12,16},{16,20},{20,24},{24,28},{28,32},{32,36}... | collective-permute-start | bytes 196616 | tf_op jit(solution)/shard_map/ppermute | solution.py:20
  125.4 104.1 %collective-permute-start.1 = (bf16[128,1,256]{2,0,1:T(8,128)(2,1)S(1)}, bf16[128,1,256]{2,0,1:T(8,128)(2,1)S(1)}, u32[]{:S(2)}, u32[]{:S(2)}) collective-permute-start(bf16[128,1,256]{2,0,1:T(8,128)(2,1)S(1)} %get-tuple-element.64), channel_id=1, source_target_pairs={{4,0},{8,4},{12,8},{16,12},{20,16},{24,20},{28,24},{32,28},{36,32}... | collective-permute-start | bytes 196616 | tf_op jit(solution)/shard_map/ppermute | solution.py:22
  229.5 10.2 %collective-permute-start.2 = (bf16[1,10,256]{2,0,1:T(2,128)(2,1)S(1)}, bf16[1,10,256]{2,0,1:T(2,128)(2,1)S(1)}, u32[]{:S(2)}, u32[]{:S(2)}) collective-permute-start(bf16[1,10,256]{2,0,1:T(2,128)(2,1)S(1)} %get-tuple-element.60), channel_id=1, source_target_pairs={{1,0},{2,1},{3,2},{5,4},{6,5},{7,6},{9,8},{10,9},{11,10},{13,12},{... | collective-permute-start | bytes 15368 | tf_op jit(solution)/shard_map/ppermute | solution.py:22
  232.1 8.3 %collective-permute-start.3 = (bf16[1,10,256]{2,0,1:T(2,128)(2,1)S(1)}, bf16[1,10,256]{2,0,1:T(2,128)(2,1)S(1)}, u32[]{:S(2)}, u32[]{:S(2)}) collective-permute-start(bf16[1,10,256]{2,0,1:T(2,128)(2,1)S(1)} %get-tuple-element.59), channel_id=1, source_target_pairs={{0,1},{1,2},{2,3},{4,5},{5,6},{6,7},{8,9},{9,10},{10,11},{12,13},{... | collective-permute-start | bytes 15368 | tf_op jit(solution)/shard_map/ppermute | solution.py:20
  236.7 5.9 collective-permute-start.4
  240.8 6.5 copy-start
  240.8 6.5 copy-start.3
  240.8 6.5 copy-start.4
  242.3 1.0 copy-start.2
  249.2 6.1 collective-permute-start.6
  253.4 9.8 %collective-permute-start.5 = (bf16[128,1,256]{2,0,1:T(8,128)(2,1)S(1)}, bf16[128,1,256]{2,0,1:T(8,128)(2,1)S(1)}, u32[]{:S(2)}, u32[]{:S(2)}) collective-permute-start(bf16[128,1,256]{2,0,1:T(8,128)(2,1)S(1)} %get-tuple-element.62), channel_id=1, source_target_pairs={{0,4},{4,8},{8,12},{12,16},{16,20},{20,24},{24,28},{28,32},{32,36}... | collective-permute-start | bytes 196616 | tf_op jit(solution)/shard_map/ppermute | solution.py:20
  263.4 9.8 %collective-permute-start.7 = (bf16[2,10,256]{2,0,1:T(2,128)(2,1)S(1)}, bf16[2,10,256]{2,0,1:T(2,128)(2,1)S(1)}, u32[]{:S(2)}, u32[]{:S(2)}) collective-permute-start(bf16[2,10,256]{2,0,1:T(2,128)(2,1)S(1)} %pad_maximum_fusion.11), channel_id=1, source_target_pairs={{0,256},{4,260},{8,264},{12,268},{16,272},{20,276},{24,280},{28,28... | collective-permute-start | bytes 30728 | tf_op jit(solution)/shard_map/ppermute | solution.py:32
  265.3 7.3 collective-permute-start.9
  267.6 5.6 collective-permute-start.8
Sparse Core Ops, SparseCore 0:
  290.8 472.8 all-reduce.2
where the time goes:
time: 775 us; the launch traced here: 774 us
  waiting for transfers between devices  379 us (49%)
  blocking collectives  309 us (40%)
  starting transfers between devices  33 us (4%)
  local copies, waits for them, and re-layouts  20.6 us (3%)
  between operations  14.5 us (2%)
  other arithmetic  11.3 us (1%)
    psum x1, waiting for transfers between devices, local(): kernel_total = lax.psum(local_kernel, ('lon', 'lat'))  370 us
    psum x1, blocking collectives, local(): lax.psum(group_total(channel_sum, GROUPS), ('lon', 'lat')) / group_cells  110 us
    psum x1, blocking collectives, local(): lax.psum((jnp.sum(normed_grad, axis=(0, 1)), jnp.sum(normed_grad * standa...  101 us
    psum x1, blocking collectives, local(): group_var = lax.psum(spread, ('lon', 'lat')) / group_cells  98.6 us
  transfers between devices with their start and end apart: 11, of which 4 were waited for; matrix products, arithmetic and copies ran while one was open for 1% of the time, Pallas kernels for 0%

commit v1 on v0

v1 whole, which is shorter than its diff:
```python
import jax
import jax.numpy as jnp
from jax import lax
from jax.experimental import pallas as pl
from jax.experimental.pallas import tpu as pltpu
from jax.sharding import PartitionSpec as P

MESH = pl.DeviceIdType.MESH
F32 = jnp.float32
BF16 = jnp.bfloat16

GROUP = 8
EPS = 1e-06
CH = 256
ROWS, COLS = 128, 8
CELLS = ROWS * COLS
ALL_CELLS = 512 * 1024
PARTS = 3
RED = 32
PIECE = 9 * CH // PARTS // RED
BLOCKS = 8
BLOCK = CELLS // BLOCKS


def ring(d, n):
    return min(d, n - d)


PLANE = sorted(
    [(dx, dy, dc) for dx in range(4) for dy in range(4) for dc in range(2)][1:],
    key=lambda d: -(ring(d[0], 4) + ring(d[1], 4) + 0.1 * d[2]),
)
COLUMN = sorted(range(1, 16), key=lambda d: -ring(d, 16))
SLAB = sorted(
    [(dx, dy, dz) for dx in range(4) for dy in range(4) for dz in range(2)][1:],
    key=lambda d: -(ring(d[0], 4) + ring(d[1], 4) + d[2]),
)
EVERY_OTHER = sorted(range(1, 8), key=lambda d: -ring(d, 8))


def device(x, y, z, c):
    return ((x * 16 + z) * 2 + lax.rem(y, 2), lax.div(y, 2) * 2 + c)


def wrapped(a, d, n):
    return lax.rem(a + d, n)


def over_group(v):
    lane = lax.broadcasted_iota(jnp.int32, v.shape, 1)
    for s in (1, 2, 4):
        up = pltpu.roll(v, 128 - s, 1)
        down = pltpu.roll(v, s, 1)
        v = v + jnp.where(lax.rem(lax.div(lane, s), 2) == 0, up, down)
    return v


def row(v):
    return jnp.concatenate([v[0:1], v[1:2]], axis=1)


def main_kernel(
    feat_hbm, cot_hbm, w_hbm, gain_hbm, shift_hbm,
    fg_hbm, kg_hbm, sums_hbm,
    xv, cv, wv, gv, sv, fgv,
    stage, even, odd, pole, hg, st, ds, ht,
    edge_out, edge_in, rows_out, rows_in, turn_in,
    pay1, in1, pay2, in2, spay1, sin1, spay2, sin2, sumsv,
    own, core_out, core_in, cut, cut_in, mid, mid_in, whole, whole_other,
    load_sem, out_sem, edge_s, edge_r, rows_s, rows_r,
    st_s, st_r, core_s, core_r, cut_s, cut_r, mid_s, mid_r, who_s, who_r, oth_s, oth_r,
):
    lon = lax.axis_index("lon")
    lat = lax.axis_index("lat")
    x = lax.div(lon, 32)
    z = lax.rem(lax.div(lon, 2), 16)
    y = lax.div(lat, 2) * 2 + lax.rem(lon, 2)
    c = lax.rem(lat, 2)
    zh = lax.div(z, 2)
    zl = lax.rem(z, 2)
    plane_rank = (x * 4 + y) * 2 + c
    slab_rank = (x * 4 + y) * 2 + zl
    at_top = lat == 0
    at_bottom = lat == 3
    east = (wrapped(lon, 1, 128), lat)
    west = (wrapped(lon, 127, 128), lat)
    south = (lon, wrapped(lat, 1, 4))
    north = (lon, wrapped(lat, 3, 4))
    half_turn = (wrapped(lon, 64, 128), lat)
    other_core = (lon, lat + 1 - 2 * c)

    def plane_peers():
        for dx, dy, dc in PLANE:
            yield device(wrapped(x, dx, 4), wrapped(y, dy, 4), z, lax.rem(c + dc, 2))

    def column_peers():
        for dz in COLUMN:
            yield device(x, y, wrapped(z, dz, 16), c)

    def send(src, dst, s, r, to):
        pltpu.make_async_remote_copy(
            src_ref=src, dst_ref=dst, send_sem=s, recv_sem=r,
            device_id=to, device_id_type=MESH,
        ).start()

    def take(ref, sem):
        pltpu.make_async_copy(ref, ref, sem).wait()

    def get(b, start, size):
        at = pl.ds(start, size)
        return jnp.concatenate([stage[b, 0, at, :], stage[b, 1, at, :]], axis=1)

    def put(b, start, v):
        at = pl.ds(start, v.shape[0])
        stage[b, 0, at, :] = v[:, :128]
        stage[b, 1, at, :] = v[:, 128:]

    loads = [
        pltpu.make_async_copy(src, dst, load_sem.at[i])
        for i, (src, dst) in enumerate(
            ((feat_hbm, xv), (cot_hbm, cv), (w_hbm, wv), (gain_hbm, gv), (shift_hbm, sv))
        )
    ]
    for load in loads:
        load.start()

    barrier = pltpu.get_barrier_semaphore()
    greeted = list(plane_peers()) + list(column_peers())
    for dx, dy, dz in SLAB:
        if dz == 1 and (dx, dy) != (0, 0):
            greeted.append(
                device(wrapped(x, dx, 4), wrapped(y, dy, 4), z + 1 - 2 * zl, c)
            )
    greeted += [east, west]
    for peer in greeted:
        pl.semaphore_signal(barrier, inc=1, device_id=peer, device_id_type=MESH)

    loads[0].wait()

    def add_up(i, acc):
        return acc + jnp.sum(xv[pl.ds(i * 16, 16)].astype(F32), axis=0)

    zero = jnp.zeros((COLS, CH), F32)
    total = lax.fori_loop(0, 8, add_up, zero, unroll=True)
    mean = jnp.sum(total, axis=0, keepdims=True) * (1.0 / CELLS)

    def spread(i, acc):
        d = xv[pl.ds(i * 16, 16)].astype(F32) - mean.reshape(1, 1, CH)
        return acc + jnp.sum(d * d, axis=0)

    total = lax.fori_loop(0, 8, spread, zero, unroll=True)
    dev = jnp.sum(total, axis=0, keepdims=True)
    pay1[0:1] = mean[:, :128]
    pay1[1:2] = mean[:, 128:]
    pay1[2:3] = dev[:, :128]
    pay1[3:4] = dev[:, 128:]
    in1[plane_rank] = pay1[...]

    pl.semaphore_wait(barrier, len(greeted))
    for peer in plane_peers():
        send(pay1, in1.at[plane_rank], st_s.at[0], st_r.at[0], peer)

    loads[1].wait()
    for i in range(BLOCKS):
        put(1, 8 + i * BLOCK, cv[pl.ds(i * 16, 16)].astype(F32).reshape(BLOCK, CH))
    for half in range(2):
        lanes = pl.ds(half * 128, 128)
        for side, col in ((0, 7), (1, 0)):
            v = stage[1, half, pl.ds(8 + col, ROWS, stride=8), :]
            edge_out[side, :, lanes] = v.astype(BF16)
    send(edge_out.at[0], edge_in.at[0], edge_s.at[0], edge_r.at[0], east)
    send(edge_out.at[1], edge_in.at[1], edge_s.at[1], edge_r.at[1], west)

    take(in1.at[pl.ds(0, 31)], st_r.at[0])
    v = in1[...]
    total = jnp.sum(v, axis=0)
    avg = total * (1.0 / 32)
    d = v - avg[None]
    sq = jnp.sum(d * d, axis=0)
    pay2[0:2] = avg[0:2]
    pay2[2:4] = total[2:4] + float(CELLS) * sq[0:2]
    in2[z] = pay2[...]
    for peer in column_peers():
        send(pay2, in2.at[z], st_s.at[1], st_r.at[1], peer)

    for i in range(BLOCKS):
        lo = 8 + i * BLOCK
        v = get(1, lo, BLOCK)
        even[1, pl.ds(i * BLOCK, BLOCK), :] = v.astype(BF16)
        put(2, lo, pltpu.roll(v, 1, 0))
        put(0, lo, pltpu.roll(v, BLOCK - 1, 0))
    take(edge_in.at[0], edge_r.at[0])
    take(edge_in.at[1], edge_r.at[1])
    for half in range(2):
        lanes = pl.ds(half * 128, 128)
        for b, side, col in ((2, 0, 0), (0, 1, 7)):
            v = edge_in[side, :, lanes].astype(F32)
            stage[b, half, pl.ds(8 + col, ROWS, stride=8), :] = v
    for b in range(3):
        rows_out[0, b] = get(b, 8, 8)
        rows_out[1, b] = get(b, CELLS, 8)
    send(rows_out.at[0], rows_in.at[1], rows_s.at[0], rows_r.at[0], north)
    send(rows_out.at[1], rows_in.at[0], rows_s.at[1], rows_r.at[1], south)
    send(rows_out, turn_in, rows_s.at[2], rows_r.at[2], half_turn)
    for b in (0, 2):
        even[b] = get(b, 8, CELLS).astype(BF16)
    pole[...] = jnp.zeros_like(pole)
    take(rows_in.at[1], rows_r.at[0])
    take(rows_in.at[0], rows_r.at[1])
    take(turn_in, rows_r.at[2])
    for b in range(3):
        put(b, 0, jnp.where(at_top, 0.0, rows_in[0, b]))
        put(b, 8 + CELLS, jnp.where(at_bottom, 0.0, rows_in[1, b]))
        odd[b] = get(b, 0, CELLS + 16).astype(BF16)
        pole[b, pl.ds(0, 16), :] = jnp.concatenate(
            [
                jnp.where(at_top, turn_in[0, b], 0.0),
                jnp.where(at_bottom, turn_in[1, b], 0.0),
            ],
            axis=0,
        ).astype(BF16)

    def window(a, b, start, size):
        if a == 0:
            return odd[b, pl.ds(16 + start, size), :]
        if a == 1:
            return even[b, pl.ds(start, size), :]
        return odd[b, pl.ds(start, size), :]

    loads[2].wait()
    contract_last = (((1,), (1,)), ((), ()))
    for i in range(4):
        acc = None
        for a in range(3):
            for b in range(3):
                part = lax.dot_general(
                    window(a, b, i * 256, 256), wv[a * 3 + b], contract_last,
                    preferred_element_type=F32,
                )
                acc = part if acc is None else acc + part
        hg[pl.ds(i * 256, 256), :] = acc
    for a, at in ((0, 0), (2, 1)):
        acc = None
        for b in range(3):
            part = lax.dot_general(
                pole[b, pl.ds(0, 16), :], wv[a * 3 + b], contract_last,
                preferred_element_type=F32,
            )
            acc = part if acc is None else acc + part
        where = pl.ds(0, 8) if at == 0 else pl.ds(CELLS - 8, 8)
        hg[where, :] = hg[where, :] + acc[at * 8 : at * 8 + 8]

    loads[3].wait()
    loads[4].wait()
    take(in2.at[pl.ds(0, 15)], st_r.at[1])
    v = in2[...]
    total = jnp.sum(v, axis=0)
    avg = total * (1.0 / 16)
    d = v - avg[None]
    sq = jnp.sum(d * d, axis=0)
    ch_mean = avg[0:2]
    ch_dev = total[2:4] + float(CELLS * 32) * sq[0:2]
    g_mean = over_group(ch_mean) * (1.0 / GROUP)
    off = ch_mean - g_mean
    g_var = over_group(ch_dev + float(ALL_CELLS) * off * off) * (
        1.0 / (GROUP * ALL_CELLS)
    )
    inv = row(1.0 / jnp.sqrt(g_var + EPS))
    mean = row(g_mean)
    gain = gv[...].reshape(1, CH)
    shift = sv[...].reshape(1, CH)

    for i in range(BLOCKS):
        at = pl.ds(i * BLOCK, BLOCK)
        s0 = (xv[pl.ds(i * 16, 16)].astype(F32).reshape(BLOCK, CH) - mean) * inv
        nm = s0 * gain + shift
        s = 1.0 / (1.0 + jnp.exp(jnp.minimum(-nm, 87.0)))
        h = (nm * s).astype(BF16)
        st[at, :] = s0
        ds[at, :] = s * (1.0 + nm * (1.0 - s))
        ht[:, at] = h.T
        if i == 0:
            first = h[0:16]
        if i == BLOCKS - 1:
            last = h[BLOCK - 16 : BLOCK]
    keep = lax.broadcasted_iota(jnp.int32, (128, CH), 0)
    zeros = jnp.zeros((112, CH), BF16)
    first = jnp.concatenate([first, zeros], axis=0).astype(F32)
    last = jnp.concatenate([last, zeros], axis=0).astype(F32)
    first_t = jnp.where(keep < 8, first, 0.0).astype(BF16).T
    last_t = jnp.where((keep >= 8) & (keep < 16), last, 0.0).astype(BF16).T

    def partial(p):
        for b in range(3):
            r = jnp.dot(ht[...], window(p, b, 0, CELLS), preferred_element_type=F32)
            if p == 0:
                r = r + jnp.dot(first_t, pole[b], preferred_element_type=F32)
            if p == 2:
                r = r + jnp.dot(last_t, pole[b], preferred_element_type=F32)
            at = pl.ds(b * CH, CH)
            own[p, at, :] = jnp.where(c == 0, r[:, :128], r[:, 128:])
            core_out[p, at, :] = jnp.where(c == 0, r[:, 128:], r[:, :128]).astype(BF16)
        send(core_out.at[p], core_in.at[p], core_s.at[p], core_r.at[p], other_core)

    def scatter(p):
        take(core_in.at[p], core_r.at[p])
        v = own[p] + core_in[p].astype(F32)
        cut[p] = v.reshape(RED, PIECE, 128).astype(BF16)
        cut_in[p, slab_rank] = cut[p, slab_rank]
        for dx, dy, dz in SLAB:
            px, py = wrapped(x, dx, 4), wrapped(y, dy, 4)
            pz = lax.rem(zl + dz, 2)
            rank = (px * 4 + py) * 2 + pz
            send(
                cut.at[p, rank], cut_in.at[p, slab_rank], cut_s.at[p], cut_r.at[p],
                device(px, py, zh * 2 + pz, c),
            )

    def exchange(p):
        take(cut_in.at[p, pl.ds(0, RED - 1)], cut_r.at[p])
        v = jnp.sum(cut_in[p].astype(F32), axis=0).astype(BF16)
        mid[p] = v
        mid_in[p, zh] = v
        for d in EVERY_OTHER:
            send(
                mid.at[p], mid_in.at[p, zh], mid_s.at[p], mid_r.at[p],
                device(x, y, wrapped(zh, d, 8) * 2 + zl, c),
            )

    def gather(p):
        take(mid_in.at[p, pl.ds(0, 7)], mid_r.at[p])
        v = jnp.sum(mid_in[p].astype(F32), axis=0) * (1.0 / ALL_CELLS)
        whole[p, slab_rank] = v.astype(BF16)
        for dx, dy, dz in SLAB:
            px, py = wrapped(x, dx, 4), wrapped(y, dy, 4)
            send(
                whole.at[p, slab_rank], whole.at[p, slab_rank], who_s.at[p], who_r.at[p],
                device(px, py, zh * 2 + lax.rem(zl + dz, 2), c),
            )

    def hand_over(p):
        take(whole.at[p, pl.ds(0, RED - 1)], who_r.at[p])
        send(whole.at[p], whole_other.at[p], oth_s.at[p], oth_r.at[p], other_core)
        pltpu.make_async_copy(whole.at[p], kg_hbm.at[p, c], out_sem.at[p]).start()

    partial(0)
    partial(1)
    scatter(0)
    partial(2)
    scatter(1)
    scatter(2)

    acc1 = zero
    acc2 = zero
    for i in range(BLOCKS):
        at = pl.ds(i * BLOCK, BLOCK)
        ng = hg[at, :] * ds[at, :]
        hg[at, :] = ng
        acc1 = acc1 + jnp.sum(ng.reshape(16, 8, CH), axis=0)
        acc2 = acc2 + jnp.sum((ng * st[at, :]).reshape(16, 8, CH), axis=0)
    s1 = jnp.sum(acc1, axis=0, keepdims=True)
    s2 = jnp.sum(acc2, axis=0, keepdims=True)
    spay1[0:1] = s1[:, :128]
    spay1[1:2] = s1[:, 128:]
    spay1[2:3] = s2[:, :128]
    spay1[3:4] = s2[:, 128:]
    sin1[plane_rank] = spay1[...]
    for peer in plane_peers():
        send(spay1, sin1.at[plane_rank], st_s.at[2], st_r.at[2], peer)

    exchange(0)
    exchange(1)
    take(sin1.at[pl.ds(0, 31)], st_r.at[2])
    spay2[...] = jnp.sum(sin1[...], axis=0)
    sin2[z] = spay2[...]
    for peer in column_peers():
        send(spay2, sin2.at[z], st_s.at[3], st_r.at[3], peer)
    exchange(2)
    for p in range(PARTS):
        gather(p)

    take(sin2.at[pl.ds(0, 15)], st_r.at[3])
    grads = jnp.sum(sin2[...], axis=0) * (1.0 / ALL_CELLS)
    sumsv[...] = grads
    to_sums = pltpu.make_async_copy(sumsv, sums_hbm, out_sem.at[PARTS])
    to_sums.start()
    gain2 = jnp.concatenate([gain[:, :128], gain[:, 128:]], axis=0)
    m1 = row(over_group(gain2 * grads[0:2]) * (1.0 / GROUP))
    m2 = row(over_group(gain2 * grads[2:4]) * (1.0 / GROUP))
    for i in range(BLOCKS):
        at = pl.ds(i * BLOCK, BLOCK)
        v = inv * (hg[at, :] * gain - m1 - st[at, :] * m2)
        fgv[pl.ds(i * 16, 16)] = v.reshape(16, 8, CH).astype(BF16)
    to_fg = pltpu.make_async_copy(fgv, fg_hbm, out_sem.at[PARTS + 1])
    to_fg.start()

    for p in range(PARTS):
        hand_over(p)
    outs = []
    for p in range(PARTS):
        take(whole_other.at[p], oth_r.at[p])
        out = pltpu.make_async_copy(
            whole_other.at[p], kg_hbm.at[p, 1 - c], out_sem.at[PARTS + 2 + p]
        )
        out.start()
        outs.append(out)

    take(edge_out.at[0], edge_s.at[0])
    take(edge_out.at[1], edge_s.at[1])
    take(rows_out.at[0], rows_s.at[0])
    take(rows_out.at[1], rows_s.at[1])
    take(rows_out, rows_s.at[2])
    take(in1.at[pl.ds(0, 31)], st_s.at[0])
    take(in2.at[pl.ds(0, 15)], st_s.at[1])
    take(sin1.at[pl.ds(0, 31)], st_s.at[2])
    take(sin2.at[pl.ds(0, 15)], st_s.at[3])
    for p in range(PARTS):
        take(core_out.at[p], core_s.at[p])
        take(cut.at[p, pl.ds(0, RED - 1)], cut_s.at[p])
        take(mid_in.at[p, pl.ds(0, 7)], mid_s.at[p])
        take(whole.at[p, pl.ds(0, RED - 1)], who_s.at[p])
        take(whole.at[p], oth_s.at[p])
        pltpu.make_async_copy(whole.at[p], kg_hbm.at[p, c], out_sem.at[p]).wait()
    to_sums.wait()
    to_fg.wait()
    for out in outs:
        out.wait()


def last_kernel(kg, fg_hbm, sums, kgrad, fg_out, gain_grad, shift_grad, sem):
    copy = pltpu.make_async_copy(fg_hbm, fg_out, sem)

    @pl.when(pl.program_id(0) == 0)
    def _():
        copy.start()
        for half in range(2):
            at = pl.ds(half * 128, 128)
            shift_grad[at] = sums[half]
            gain_grad[at] = sums[2 + half]

    for half in range(2):
        v = kg[0, half].astype(F32).reshape(RED * PIECE, 128)
        kgrad[:, pl.ds(half * 128, 128)] = v

    @pl.when(pl.program_id(0) == PARTS - 1)
    def _():
        copy.wait()


def local(features, cotangent, kernel, norm_gain, norm_shift):
    any_spec = pl.BlockSpec(memory_space=pl.ANY)
    vmem = pltpu.VMEM
    dma = pltpu.SemaphoreType.DMA
    features, cotangent, kernel, norm_gain, norm_shift = [
        pltpu.with_memory_space_constraint(v, pltpu.HBM)
        for v in (features, cotangent, kernel.reshape(9, CH, CH), norm_gain, norm_shift)
    ]
    fg, kg, sums = pl.pallas_call(
        main_kernel,
        out_shape=(
            jax.ShapeDtypeStruct((ROWS, COLS, CH), BF16),
            jax.ShapeDtypeStruct((PARTS, 2, RED, PIECE, 128), BF16),
            jax.ShapeDtypeStruct((4, 128), F32),
        ),
        in_specs=[pl.BlockSpec(memory_space=pltpu.HBM)] * 5,
        out_specs=(any_spec,) * 3,
        scratch_shapes=[
            vmem((ROWS, COLS, CH), BF16),
            vmem((ROWS, COLS, CH), BF16),
            vmem((9, CH, CH), BF16),
            vmem((CH,), F32),
            vmem((CH,), F32),
            vmem((ROWS, COLS, CH), BF16),
            vmem((3, 2, CELLS + 16, 128), F32),
            vmem((3, CELLS, CH), BF16),
            vmem((3, CELLS + 16, CH), BF16),
            vmem((3, 128, CH), BF16),
            vmem((CELLS, CH), F32),
            vmem((CELLS, CH), F32),
            vmem((CELLS, CH), F32),
            vmem((CH, CELLS), BF16),
            vmem((2, ROWS, CH), BF16),
            vmem((2, ROWS, CH), BF16),
            vmem((2, 3, 8, CH), F32),
            vmem((2, 3, 8, CH), F32),
            vmem((2, 3, 8, CH), F32),
            vmem((4, 128), F32),
            vmem((32, 4, 128), F32),
            vmem((4, 128), F32),
            vmem((16, 4, 128), F32),
            vmem((4, 128), F32),
            vmem((32, 4, 128), F32),
            vmem((4, 128), F32),
            vmem((16, 4, 128), F32),
            vmem((4, 128), F32),
            vmem((PARTS, RED * PIECE, 128), F32),
            vmem((PARTS, RED * PIECE, 128), BF16),
            vmem((PARTS, RED * PIECE, 128), BF16),
            vmem((PARTS, RED, PIECE, 128), BF16),
            vmem((PARTS, RED, PIECE, 128), BF16),
            vmem((PARTS, PIECE, 128), BF16),
            vmem((PARTS, 8, PIECE, 128), BF16),
            vmem((PARTS, RED, PIECE, 128), BF16),
            vmem((PARTS, RED, PIECE, 128), BF16),
            dma((5,)),
            dma((2 * PARTS + 2,)),
            dma((2,)), dma((2,)),
            dma((3,)), dma((3,)),
            dma((4,)), dma((4,)),
            dma((PARTS,)), dma((PARTS,)),
            dma((PARTS,)), dma((PARTS,)),
            dma((PARTS,)), dma((PARTS,)),
            dma((PARTS,)), dma((PARTS,)),
            dma((PARTS,)), dma((PARTS,)),
        ],
        compiler_params=pltpu.CompilerParams(
            collective_id=0, has_side_effects=True, vmem_limit_bytes=48 * 2**20
        ),
        name="backward",
    )(features, cotangent, kernel, norm_gain, norm_shift)
    kgrad, fg, gain_grad, shift_grad = pl.pallas_call(
        last_kernel,
        grid=(PARTS,),
        out_shape=(
            jax.ShapeDtypeStruct((9 * CH, CH), F32),
            jax.ShapeDtypeStruct((ROWS, COLS, CH), BF16),
            jax.ShapeDtypeStruct((CH,), F32),
            jax.ShapeDtypeStruct((CH,), F32),
        ),
        in_specs=[
            pl.BlockSpec((1, 2, RED, PIECE, 128), lambda i: (i, 0, 0, 0, 0)),
            any_spec,
            pl.BlockSpec((4, 128), lambda i: (0, 0)),
        ],
        out_specs=(
            pl.BlockSpec((RED * PIECE, CH), lambda i: (i, 0)),
            any_spec,
            pl.BlockSpec((CH,), lambda i: (0,)),
            pl.BlockSpec((CH,), lambda i: (0,)),
        ),
        scratch_shapes=[dma],
        compiler_params=pltpu.CompilerParams(vmem_limit_bytes=16 * 2**20),
        name="outputs",
    )(kg, fg, sums)
    return fg, kgrad.reshape(3, 3, CH, CH), gain_grad, shift_grad


def solution(mesh):
    placed = (P("lat", "lon", None), P("lat", "lon", None), P(), P(), P())
    return jax.shard_map(
        local,
        mesh=mesh,
        in_specs=placed,
        out_specs=(P("lat", "lon", None), P(), P(), P()),
        check_vma=False,
    )
```

time: 775 us -> 63.1 us (0.08)
  waiting for transfers between devices: 379 us -> 0 us
  blocking collectives: 309 us -> 0 us
  Pallas kernels: 0 us -> 62.3 us
  starting transfers between devices: 33 us -> 0 us
  local copies, waits for them, and re-layouts: 20.6 us -> 0 us
  between operations: 14.5 us -> 0.64 us
  other arithmetic: 11.3 us -> 0 us
    psum x1 -> x0, waiting for transfers between devices: 370 us -> none  [local(): kernel_total = lax.psum(local_kernel, ('lon', 'lat'))]
    psum x3 -> x0, blocking collectives: 309 us -> none  [the longest x1 110 us: local(): lax.psum(group_total(channel_sum, GROUPS), ('lon', 'lat')) / group_cells]
    pallas_call x0 -> x2, Pallas kernels: none -> 62.3 us  [the longest x1 60.3 us: local(): pl.pallas_call(main_kernel, out_shape=(jax.ShapeDtypeStruct((ROWS, COLS,...]
    ppermute x10 -> x0, starting transfers between devices: 33 us -> none  [the longest x4 15.4 us: with_halo(): lax.ppermute(tail, axis, [(i, (i + 1) % count) for i in range(ends)])]
    ppermute x10 -> x0, waiting for transfers between devices: 8.83 us -> none  [the longest x4 8.51 us: with_halo(): lax.ppermute(tail, axis, [(i, (i + 1) % count) for i in range(ends)])]
  transfers between devices with their start and end apart: 11 -> 0, of which waited for: 4 -> 0; matrix products, arithmetic and copies ran while one was open for 1% -> 0% of each run, Pallas kernels for 0% -> 0%
where the time goes in v1:
time: 63.1 us; the launch traced here: 63 us
  Pallas kernels  62.3 us (99%)
  between operations  0.64 us (1%)
    pallas_call x1, Pallas kernels, local(): pl.pallas_call(main_kernel, out_shape=(jax.ShapeDtypeStruct((ROWS, COLS,...  60.3 us
    pallas_call x1, Pallas kernels, local(): pl.pallas_call(last_kernel, grid=(PARTS,), out_shape=(jax.ShapeDtypeStruc...  2.03 us

profile of v1, /device:TPU:1, one launch (start us, length us, event | category | flops | bytes accessed | tf_op | source)
XLA Modules:
  0.0 63.0 jit_solution(4516673615691254100)
XLA Ops:
  0.6 60.3 %backward.1 = (bf16[128,8,256]{2,1,0:T(8,128)(2,1)S(1)}, bf16[3,2,32,24,128]{4,3,2,1,0:T(8,128)(2,1)S(1)}, f32[4,128]{1,0:T(4,128)S(1)}) custom-call(bf16[128,8,256]{2,1,0:T(8,128)(2,1)} %feat_hbm.1, bf16[128,8,256]{2,1,0:T(8,128)(2,1)} %cot_hbm.1, bf16[9,256,256]{2,1,0:T(8,128)(2,1)} %bitcast.2, f32[256]{0:T(256)} %gain_hbm.1, f32[256]{0:T(256)} %shift_hbm.1), custom_call_target="tpu_custom_call" | custom-call | tf_op jit(solution)/shard_map/backward/pallas_call | solution.py:458
  60.9 2.0 %outputs.1 = (f32[2304,256]{1,0:T(8,128)}, bf16[128,8,256]{2,1,0:T(8,128)(2,1)}, f32[256]{0:T(256)}, f32[256]{0:T(256)}) custom-call(bf16[3,2,32,24,128]{4,3,2,1,0:T(8,128)(2,1)S(1)} %get-tuple-element.11.kg, bf16[128,8,256]{2,1,0:T(8,128)(2,1)S(1)} %get-tuple-element.12.fg_hbm, f32[4,128]{1,0:T(4,128)S(1)} %get-tuple-element.13.sums), custom_call_target="tpu_custom_call" | custom-call | tf_op jit(solution)/shard_map/outputs/pallas_call | solution.py:521

commit v2 on v1

--- a/solution.py
+++ b/solution.py
@@ -63,11 +63,11 @@
     feat_hbm, cot_hbm, w_hbm, gain_hbm, shift_hbm,
     fg_hbm, kg_hbm, sums_hbm,
     xv, cv, wv, gv, sv, fgv,
-    stage, even, odd, pole, hg, st, ds, ht,
+    stage, even, odd, pole, hg, ht,
     edge_out, edge_in, rows_out, rows_in, turn_in,
     pay1, in1, pay2, in2, spay1, sin1, spay2, sin2, sumsv,
     own, core_out, core_in, cut, cut_in, mid, mid_in, whole, whole_other,
-    load_sem, out_sem, edge_s, edge_r, rows_s, rows_r,
+    relay_sem, load_sem, out_sem, edge_s, edge_r, rows_s, rows_r,
     st_s, st_r, core_s, core_r, cut_s, cut_r, mid_s, mid_r, who_s, who_r, oth_s, oth_r,
 ):
     lon = lax.axis_index("lon")
@@ -121,19 +121,22 @@
             ((feat_hbm, xv), (cot_hbm, cv), (w_hbm, wv), (gain_hbm, gv), (shift_hbm, sv))
         )
     ]
-    for load in loads:
-        load.start()
+    loads[0].start()
 
     barrier = pltpu.get_barrier_semaphore()
-    greeted = list(plane_peers()) + list(column_peers())
+    greeted = [device(x, y, wrapped(z, d, 16), c) for d in (4, 12)]
     for dx, dy, dz in SLAB:
         if dz == 1 and (dx, dy) != (0, 0):
             greeted.append(
                 device(wrapped(x, dx, 4), wrapped(y, dy, 4), z + 1 - 2 * zl, c)
             )
+    greeted += list(plane_peers())
+    greeted += [device(x, y, wrapped(z, d, 16), c) for d in (3, 13, 2, 14, 1, 15)]
     greeted += [east, west]
     for peer in greeted:
         pl.semaphore_signal(barrier, inc=1, device_id=peer, device_id_type=MESH)
+    for load in loads[1:]:
+        load.start()
 
     loads[0].wait()
 
@@ -157,6 +160,11 @@
     in1[plane_rank] = pay1[...]
 
     pl.semaphore_wait(barrier, len(greeted))
+    for d in (4, 12):
+        pl.semaphore_signal(
+            relay_sem, inc=1, device_id=device(x, y, wrapped(z, d, 16), c),
+            device_id_type=MESH,
+        )
     for peer in plane_peers():
         send(pay1, in1.at[plane_rank], st_s.at[0], st_r.at[0], peer)
 
@@ -180,6 +188,7 @@
     pay2[0:2] = avg[0:2]
     pay2[2:4] = total[2:4] + float(CELLS) * sq[0:2]
     in2[z] = pay2[...]
+    pl.semaphore_wait(relay_sem, 2)
     for peer in column_peers():
         send(pay2, in2.at[z], st_s.at[1], st_r.at[1], peer)
 
@@ -270,14 +279,18 @@
     gain = gv[...].reshape(1, CH)
     shift = sv[...].reshape(1, CH)
 
+    def standard(i):
+        return (xv[pl.ds(i * 16, 16)].astype(F32).reshape(BLOCK, CH) - mean) * inv
+
+    def logistic(v):
+        d = 1.0 + jnp.exp(jnp.minimum(-v, 87.0))
+        r = pl.reciprocal(d, approx=True)
+        return r * (2.0 - d * r)
+
     for i in range(BLOCKS):
         at = pl.ds(i * BLOCK, BLOCK)
-        s0 = (xv[pl.ds(i * 16, 16)].astype(F32).reshape(BLOCK, CH) - mean) * inv
-        nm = s0 * gain + shift
-        s = 1.0 / (1.0 + jnp.exp(jnp.minimum(-nm, 87.0)))
-        h = (nm * s).astype(BF16)
-        st[at, :] = s0
-        ds[at, :] = s * (1.0 + nm * (1.0 - s))
+        nm = standard(i) * gain + shift
+        h = (nm * logistic(nm)).astype(BF16)
         ht[:, at] = h.T
         if i == 0:
             first = h[0:16]
@@ -354,10 +367,13 @@
     acc2 = zero
     for i in range(BLOCKS):
         at = pl.ds(i * BLOCK, BLOCK)
-        ng = hg[at, :] * ds[at, :]
+        s0 = standard(i)
+        nm = s0 * gain + shift
+        s = logistic(nm)
+        ng = hg[at, :] * (s * (1.0 + nm * (1.0 - s)))
         hg[at, :] = ng
         acc1 = acc1 + jnp.sum(ng.reshape(16, 8, CH), axis=0)
-        acc2 = acc2 + jnp.sum((ng * st[at, :]).reshape(16, 8, CH), axis=0)
+        acc2 = acc2 + jnp.sum((ng * s0).reshape(16, 8, CH), axis=0)
     s1 = jnp.sum(acc1, axis=0, keepdims=True)
     s2 = jnp.sum(acc2, axis=0, keepdims=True)
     spay1[0:1] = s1[:, :128]
@@ -370,12 +386,12 @@
 
     exchange(0)
     exchange(1)
+    exchange(2)
     take(sin1.at[pl.ds(0, 31)], st_r.at[2])
     spay2[...] = jnp.sum(sin1[...], axis=0)
     sin2[z] = spay2[...]
     for peer in column_peers():
         send(spay2, sin2.at[z], st_s.at[3], st_r.at[3], peer)
-    exchange(2)
     for p in range(PARTS):
         gather(p)
 
@@ -389,7 +405,7 @@
     m2 = row(over_group(gain2 * grads[2:4]) * (1.0 / GROUP))
     for i in range(BLOCKS):
         at = pl.ds(i * BLOCK, BLOCK)
-        v = inv * (hg[at, :] * gain - m1 - st[at, :] * m2)
+        v = inv * (hg[at, :] * gain - m1 - standard(i) * m2)
         fgv[pl.ds(i * 16, 16)] = v.reshape(16, 8, CH).astype(BF16)
     to_fg = pltpu.make_async_copy(fgv, fg_hbm, out_sem.at[PARTS + 1])
     to_fg.start()
@@ -476,8 +492,6 @@
             vmem((3, CELLS + 16, CH), BF16),
             vmem((3, 128, CH), BF16),
             vmem((CELLS, CH), F32),
-            vmem((CELLS, CH), F32),
-            vmem((CELLS, CH), F32),
             vmem((CH, CELLS), BF16),
             vmem((2, ROWS, CH), BF16),
             vmem((2, ROWS, CH), BF16),
@@ -502,6 +516,7 @@
             vmem((PARTS, 8, PIECE, 128), BF16),
             vmem((PARTS, RED, PIECE, 128), BF16),
             vmem((PARTS, RED, PIECE, 128), BF16),
+            pltpu.SemaphoreType.REGULAR,
             dma((5,)),
             dma((2 * PARTS + 2,)),
             dma((2,)), dma((2,)),

time: 63.1 us -> 59.6 us (0.945)
  Pallas kernels: 62.3 us -> 58.8 us
    pallas_call x1, Pallas kernels: 60.3 us -> 56.8 us  [local(): pl.pallas_call(main_kernel, out_shape=(jax.ShapeDtypeStruct((ROWS, COLS,...]
where the time goes in v2:
time: 59.6 us; the launch traced here: 59.4 us
  Pallas kernels  58.8 us (99%)
  between operations  0.64 us (1%)
    pallas_call x1, Pallas kernels, local(): pl.pallas_call(main_kernel, out_shape=(jax.ShapeDtypeStruct((ROWS, COLS,...  56.8 us
    pallas_call x1, Pallas kernels, local(): pl.pallas_call(last_kernel, grid=(PARTS,), out_shape=(jax.ShapeDtypeStruc...  2.03 us

profile of v2, /device:TPU:1, one launch (start us, length us, event | category | flops | bytes accessed | tf_op | source)
XLA Modules:
  0.0 59.4 jit_solution(16170201738122603809)
XLA Ops:
  0.6 56.8 %backward.1 = (bf16[128,8,256]{2,1,0:T(8,128)(2,1)S(1)}, bf16[3,2,32,24,128]{4,3,2,1,0:T(8,128)(2,1)S(1)}, f32[4,128]{1,0:T(4,128)S(1)}) custom-call(bf16[128,8,256]{2,1,0:T(8,128)(2,1)} %feat_hbm.1, bf16[128,8,256]{2,1,0:T(8,128)(2,1)} %cot_hbm.1, bf16[9,256,256]{2,1,0:T(8,128)(2,1)} %bitcast.2, f32[256]{0:T(256)} %gain_hbm.1, f32[256]{0:T(256)} %shift_hbm.1), custom_call_target="tpu_custom_call" | custom-call | tf_op jit(solution)/shard_map/backward/pallas_call | solution.py:474
  57.4 2.0 %outputs.1 = (f32[2304,256]{1,0:T(8,128)}, bf16[128,8,256]{2,1,0:T(8,128)(2,1)}, f32[256]{0:T(256)}, f32[256]{0:T(256)}) custom-call(bf16[3,2,32,24,128]{4,3,2,1,0:T(8,128)(2,1)S(1)} %get-tuple-element.11.kg, bf16[128,8,256]{2,1,0:T(8,128)(2,1)S(1)} %get-tuple-element.12.fg_hbm, f32[4,128]{1,0:T(4,128)S(1)} %get-tuple-element.13.sums), custom_call_target="tpu_custom_call" | custom-call | tf_op jit(solution)/shard_map/outputs/pallas_call | solution.py:536

commit v3 on v2

--- a/solution.py
+++ b/solution.py
@@ -15,9 +15,10 @@
 ROWS, COLS = 128, 8
 CELLS = ROWS * COLS
 ALL_CELLS = 512 * 1024
-PARTS = 3
+TAPS = ((3, 4, 5), (0, 1, 2), (6, 7, 8))
+PARTS = len(TAPS)
 RED = 32
-PIECE = 9 * CH // PARTS // RED
+PIECES = [len(taps) * CH // RED for taps in TAPS]
 BLOCKS = 8
 BLOCK = CELLS // BLOCKS
 
@@ -59,17 +60,28 @@
     return jnp.concatenate([v[0:1], v[1:2]], axis=1)
 
 
-def main_kernel(
-    feat_hbm, cot_hbm, w_hbm, gain_hbm, shift_hbm,
-    fg_hbm, kg_hbm, sums_hbm,
-    xv, cv, wv, gv, sv, fgv,
-    stage, even, odd, pole, hg, ht,
-    edge_out, edge_in, rows_out, rows_in, turn_in,
-    pay1, in1, pay2, in2, spay1, sin1, spay2, sin2, sumsv,
-    own, core_out, core_in, cut, cut_in, mid, mid_in, whole, whole_other,
-    relay_sem, load_sem, out_sem, edge_s, edge_r, rows_s, rows_r,
-    st_s, st_r, core_s, core_r, cut_s, cut_r, mid_s, mid_r, who_s, who_r, oth_s, oth_r,
-):
+def main_kernel(*refs):
+    refs = list(refs)
+
+    def several(n):
+        out = refs[:n]
+        del refs[:n]
+        return out
+
+    feat_hbm, cot_hbm, w_hbm, gain_hbm, shift_hbm, fg_hbm, sums_hbm = several(7)
+    kg_hbm = several(PARTS)
+    xv, cv, wv, gv, sv, fgv = several(6)
+    stage, even, odd, pole, hg, ht = several(6)
+    edge_out, edge_in, rows_out, rows_in, turn_in = several(5)
+    pay1, in1, pay2, in2, spay1, sin1, spay2, sin2, sumsv = several(9)
+    own, core_out, core_in, cut, cut_in, mid, mid_in, whole = [
+        several(PARTS) for _ in range(8)
+    ]
+    relay_sem, load_sem, out_sem = several(3)
+    edge_s, edge_r, rows_s, rows_r, st_s, st_r = several(6)
+    core_s, core_r, cut_s, cut_r, mid_s, mid_r = several(6)
+    who_s, who_r, oth_s, oth_r = several(4)
+
     lon = lax.axis_index("lon")
     lat = lax.axis_index("lat")
     x = lax.div(lon, 32)
@@ -176,8 +188,6 @@
         for side, col in ((0, 7), (1, 0)):
             v = stage[1, half, pl.ds(8 + col, ROWS, stride=8), :]
             edge_out[side, :, lanes] = v.astype(BF16)
-    send(edge_out.at[0], edge_in.at[0], edge_s.at[0], edge_r.at[0], east)
-    send(edge_out.at[1], edge_in.at[1], edge_s.at[1], edge_r.at[1], west)
 
     take(in1.at[pl.ds(0, 31)], st_r.at[0])
     v = in1[...]
@@ -191,6 +201,8 @@
     pl.semaphore_wait(relay_sem, 2)
     for peer in column_peers():
         send(pay2, in2.at[z], st_s.at[1], st_r.at[1], peer)
+    send(edge_out.at[0], edge_in.at[0], edge_s.at[0], edge_r.at[0], east)
+    send(edge_out.at[1], edge_in.at[1], edge_s.at[1], edge_r.at[1], west)
 
     for i in range(BLOCKS):
         lo = 8 + i * BLOCK
@@ -213,21 +225,6 @@
     send(rows_out, turn_in, rows_s.at[2], rows_r.at[2], half_turn)
     for b in (0, 2):
         even[b] = get(b, 8, CELLS).astype(BF16)
-    pole[...] = jnp.zeros_like(pole)
-    take(rows_in.at[1], rows_r.at[0])
-    take(rows_in.at[0], rows_r.at[1])
-    take(turn_in, rows_r.at[2])
-    for b in range(3):
-        put(b, 0, jnp.where(at_top, 0.0, rows_in[0, b]))
-        put(b, 8 + CELLS, jnp.where(at_bottom, 0.0, rows_in[1, b]))
-        odd[b] = get(b, 0, CELLS + 16).astype(BF16)
-        pole[b, pl.ds(0, 16), :] = jnp.concatenate(
-            [
-                jnp.where(at_top, turn_in[0, b], 0.0),
-                jnp.where(at_bottom, turn_in[1, b], 0.0),
-            ],
-            axis=0,
-        ).astype(BF16)
 
     def window(a, b, start, size):
         if a == 0:
@@ -235,6 +232,133 @@
         if a == 1:
             return even[b, pl.ds(start, size), :]
         return odd[b, pl.ds(start, size), :]
+
+    loads[3].wait()
+    loads[4].wait()
+    take(in2.at[pl.ds(0, 15)], st_r.at[1])
+    v = in2[...]
+    total = jnp.sum(v, axis=0)
+    avg = total * (1.0 / 16)
+    d = v - avg[None]
+    sq = jnp.sum(d * d, axis=0)
+    ch_mean = avg[0:2]
+    ch_dev = total[2:4] + float(CELLS * 32) * sq[0:2]
+    g_mean = over_group(ch_mean) * (1.0 / GROUP)
+    off = ch_mean - g_mean
+    g_var = over_group(ch_dev + float(ALL_CELLS) * off * off) * (
+        1.0 / (GROUP * ALL_CELLS)
+    )
+    inv = row(1.0 / jnp.sqrt(g_var + EPS))
+    mean = row(g_mean)
+    gain = gv[...].reshape(1, CH)
+    shift = sv[...].reshape(1, CH)
+
+    def standard(i):
+        return (xv[pl.ds(i * 16, 16)].astype(F32).reshape(BLOCK, CH) - mean) * inv
+
+    def logistic(v):
+        d = 1.0 + jnp.exp(jnp.minimum(-v, 87.0))
+        r = pl.reciprocal(d, approx=True)
+        return r * (2.0 - d * r)
+
+    for i in range(BLOCKS):
+        at = pl.ds(i * BLOCK, BLOCK)
+        nm = standard(i) * gain + shift
+        h = (nm * logistic(nm)).astype(BF16)
+        ht[:, at] = h.T
+        if i == 0:
+            first = h[0:16]
+        if i == BLOCKS - 1:
+            last = h[BLOCK - 16 : BLOCK]
+    keep = lax.broadcasted_iota(jnp.int32, (128, CH), 0)
+    zeros = jnp.zeros((112, CH), BF16)
+    first = jnp.concatenate([first, zeros], axis=0).astype(F32)
+    last = jnp.concatenate([last, zeros], axis=0).astype(F32)
+    first_t = jnp.where(keep < 8, first, 0.0).astype(BF16).T
+    last_t = jnp.where((keep >= 8) & (keep < 16), last, 0.0).astype(BF16).T
+
+    def partial(p):
+        for k, tap in enumerate(TAPS[p]):
+            a, b = tap // 3, tap % 3
+            r = jnp.dot(ht[...], window(a, b, 0, CELLS), preferred_element_type=F32)
+            if a == 0:
+                r = r + jnp.dot(first_t, pole[b], preferred_element_type=F32)
+            if a == 2:
+                r = r + jnp.dot(last_t, pole[b], preferred_element_type=F32)
+            at = pl.ds(k * CH, CH)
+            own[p][at, :] = jnp.where(c == 0, r[:, :128], r[:, 128:])
+            core_out[p][at, :] = jnp.where(c == 0, r[:, 128:], r[:, :128]).astype(BF16)
+        send(core_out[p], core_in[p], core_s.at[p], core_r.at[p], other_core)
+
+    def scatter(p):
+        take(core_in[p], core_r.at[p])
+        v = own[p][...] + core_in[p][...].astype(F32)
+        cut[p][...] = v.reshape(RED, PIECES[p], 128).astype(BF16)
+        cut_in[p][slab_rank] = cut[p][slab_rank]
+        for dx, dy, dz in SLAB:
+            px, py = wrapped(x, dx, 4), wrapped(y, dy, 4)
+            pz = lax.rem(zl + dz, 2)
+            rank = (px * 4 + py) * 2 + pz
+            send(
+                cut[p].at[rank], cut_in[p].at[slab_rank], cut_s.at[p], cut_r.at[p],
+                device(px, py, zh * 2 + pz, c),
+            )
+
+    def exchange(p):
+        take(cut_in[p].at[pl.ds(0, RED - 1)], cut_r.at[p])
+        v = jnp.sum(cut_in[p][...].astype(F32), axis=0).astype(BF16)
+        mid[p][...] = v
+        mid_in[p][zh] = v
+        for d in EVERY_OTHER:
+            send(
+                mid[p], mid_in[p].at[zh], mid_s.at[p], mid_r.at[p],
+                device(x, y, wrapped(zh, d, 8) * 2 + zl, c),
+            )
+
+    def gather(p):
+        take(mid_in[p].at[pl.ds(0, 7)], mid_r.at[p])
+        v = jnp.sum(mid_in[p][...].astype(F32), axis=0) * (1.0 / ALL_CELLS)
+        whole[p][slab_rank] = v.astype(BF16)
+        mine = whole[p].at[slab_rank]
+        for dx, dy, dz in SLAB:
+            px, py = wrapped(x, dx, 4), wrapped(y, dy, 4)
+            send(
+                mine, mine, who_s.at[p], who_r.at[p],
+                device(px, py, zh * 2 + lax.rem(zl + dz, 2), c),
+            )
+
+    def keep_own(p):
+        return pltpu.make_async_copy(whole[p], kg_hbm[p].at[c], out_sem.at[p])
+
+    def hand_over(p):
+        take(whole[p].at[pl.ds(0, RED - 1)], who_r.at[p])
+        send(whole[p], kg_hbm[p].at[c], oth_s.at[p], oth_r.at[p], other_core)
+        keep_own(p).start()
+
+    def rows_arrive():
+        pole[...] = jnp.zeros_like(pole)
+        take(rows_in.at[1], rows_r.at[0])
+        take(rows_in.at[0], rows_r.at[1])
+        take(turn_in, rows_r.at[2])
+        for b in range(3):
+            put(b, 0, jnp.where(at_top, 0.0, rows_in[0, b]))
+            put(b, 8 + CELLS, jnp.where(at_bottom, 0.0, rows_in[1, b]))
+            odd[b] = get(b, 0, CELLS + 16).astype(BF16)
+            pole[b, pl.ds(0, 16), :] = jnp.concatenate(
+                [
+                    jnp.where(at_top, turn_in[0, b], 0.0),
+                    jnp.where(at_bottom, turn_in[1, b], 0.0),
+                ],
+                axis=0,
+            ).astype(BF16)
+
+    partial(0)
+    scatter(0)
+    rows_arrive()
+    partial(1)
+    partial(2)
+    scatter(1)
+    scatter(2)
 
     loads[2].wait()
     contract_last = (((1,), (1,)), ((), ()))
@@ -259,110 +383,6 @@
         where = pl.ds(0, 8) if at == 0 else pl.ds(CELLS - 8, 8)
         hg[where, :] = hg[where, :] + acc[at * 8 : at * 8 + 8]
 
-    loads[3].wait()
-    loads[4].wait()
-    take(in2.at[pl.ds(0, 15)], st_r.at[1])
-    v = in2[...]
-    total = jnp.sum(v, axis=0)
-    avg = total * (1.0 / 16)
-    d = v - avg[None]
-    sq = jnp.sum(d * d, axis=0)
-    ch_mean = avg[0:2]
-    ch_dev = total[2:4] + float(CELLS * 32) * sq[0:2]
-    g_mean = over_group(ch_mean) * (1.0 / GROUP)
-    off = ch_mean - g_mean
-    g_var = over_group(ch_dev + float(ALL_CELLS) * off * off) * (
-        1.0 / (GROUP * ALL_CELLS)
-    )
-    inv = row(1.0 / jnp.sqrt(g_var + EPS))
-    mean = row(g_mean)
-    gain = gv[...].reshape(1, CH)
-    shift = sv[...].reshape(1, CH)
-
-    def standard(i):
-        return (xv[pl.ds(i * 16, 16)].astype(F32).reshape(BLOCK, CH) - mean) * inv
-
-    def logistic(v):
-        d = 1.0 + jnp.exp(jnp.minimum(-v, 87.0))
-        r = pl.reciprocal(d, approx=True)
-        return r * (2.0 - d * r)
-
-    for i in range(BLOCKS):
-        at = pl.ds(i * BLOCK, BLOCK)
-        nm = standard(i) * gain + shift
-        h = (nm * logistic(nm)).astype(BF16)
-        ht[:, at] = h.T
-        if i == 0:
-            first = h[0:16]
-        if i == BLOCKS - 1:
-            last = h[BLOCK - 16 : BLOCK]
-    keep = lax.broadcasted_iota(jnp.int32, (128, CH), 0)
-    zeros = jnp.zeros((112, CH), BF16)
-    first = jnp.concatenate([first, zeros], axis=0).astype(F32)
-    last = jnp.concatenate([last, zeros], axis=0).astype(F32)
-    first_t = jnp.where(keep < 8, first, 0.0).astype(BF16).T
-    last_t = jnp.where((keep >= 8) & (keep < 16), last, 0.0).astype(BF16).T
-
-    def partial(p):
-        for b in range(3):
-            r = jnp.dot(ht[...], window(p, b, 0, CELLS), preferred_element_type=F32)
-            if p == 0:
-                r = r + jnp.dot(first_t, pole[b], preferred_element_type=F32)
-            if p == 2:
-                r = r + jnp.dot(last_t, pole[b], preferred_element_type=F32)
-            at = pl.ds(b * CH, CH)
-            own[p, at, :] = jnp.where(c == 0, r[:, :128], r[:, 128:])
-            core_out[p, at, :] = jnp.where(c == 0, r[:, 128:], r[:, :128]).astype(BF16)
-        send(core_out.at[p], core_in.at[p], core_s.at[p], core_r.at[p], other_core)
-
-    def scatter(p):
-        take(core_in.at[p], core_r.at[p])
-        v = own[p] + core_in[p].astype(F32)
-        cut[p] = v.reshape(RED, PIECE, 128).astype(BF16)
-        cut_in[p, slab_rank] = cut[p, slab_rank]
-        for dx, dy, dz in SLAB:
-            px, py = wrapped(x, dx, 4), wrapped(y, dy, 4)
-            pz = lax.rem(zl + dz, 2)
-            rank = (px * 4 + py) * 2 + pz
-            send(
-                cut.at[p, rank], cut_in.at[p, slab_rank], cut_s.at[p], cut_r.at[p],
-                device(px, py, zh * 2 + pz, c),
-            )
-
-    def exchange(p):
-        take(cut_in.at[p, pl.ds(0, RED - 1)], cut_r.at[p])
-        v = jnp.sum(cut_in[p].astype(F32), axis=0).astype(BF16)
-        mid[p] = v
-        mid_in[p, zh] = v
-        for d in EVERY_OTHER:
-            send(
-                mid.at[p], mid_in.at[p, zh], mid_s.at[p], mid_r.at[p],
-                device(x, y, wrapped(zh, d, 8) * 2 + zl, c),
-            )
-
-    def gather(p):
-        take(mid_in.at[p, pl.ds(0, 7)], mid_r.at[p])
-        v = jnp.sum(mid_in[p].astype(F32), axis=0) * (1.0 / ALL_CELLS)
-        whole[p, slab_rank] = v.astype(BF16)
-        for dx, dy, dz in SLAB:
-            px, py = wrapped(x, dx, 4), wrapped(y, dy, 4)
-            send(
-                whole.at[p, slab_rank], whole.at[p, slab_rank], who_s.at[p], who_r.at[p],
-                device(px, py, zh * 2 + lax.rem(zl + dz, 2), c),
-            )
-
-    def hand_over(p):
-        take(whole.at[p, pl.ds(0, RED - 1)], who_r.at[p])
-        send(whole.at[p], whole_other.at[p], oth_s.at[p], oth_r.at[p], other_core)
-        pltpu.make_async_copy(whole.at[p], kg_hbm.at[p, c], out_sem.at[p]).start()
-
-    partial(0)
-    partial(1)
-    scatter(0)
-    partial(2)
-    scatter(1)
-    scatter(2)
-
     acc1 = zero
     acc2 = zero
     for i in range(BLOCKS):
@@ -384,9 +404,8 @@
     for peer in plane_peers():
         send(spay1, sin1.at[plane_rank], st_s.at[2], st_r.at[2], peer)
 
-    exchange(0)
-    exchange(1)
-    exchange(2)
+    for p in range(PARTS):
+        exchange(p)
     take(sin1.at[pl.ds(0, 31)], st_r.at[2])
     spay2[...] = jnp.sum(sin1[...], axis=0)
     sin2[z] = spay2[...]
@@ -412,14 +431,6 @@
 
     for p in range(PARTS):
         hand_over(p)
-    outs = []
-    for p in range(PARTS):
-        take(whole_other.at[p], oth_r.at[p])
-        out = pltpu.make_async_copy(
-            whole_other.at[p], kg_hbm.at[p, 1 - c], out_sem.at[PARTS + 2 + p]
-        )
-        out.start()
-        outs.append(out)
 
     take(edge_out.at[0], edge_s.at[0])
     take(edge_out.at[1], edge_s.at[1])
@@ -431,36 +442,38 @@
     take(sin1.at[pl.ds(0, 31)], st_s.at[2])
     take(sin2.at[pl.ds(0, 15)], st_s.at[3])
     for p in range(PARTS):
-        take(core_out.at[p], core_s.at[p])
-        take(cut.at[p, pl.ds(0, RED - 1)], cut_s.at[p])
-        take(mid_in.at[p, pl.ds(0, 7)], mid_s.at[p])
-        take(whole.at[p, pl.ds(0, RED - 1)], who_s.at[p])
-        take(whole.at[p], oth_s.at[p])
-        pltpu.make_async_copy(whole.at[p], kg_hbm.at[p, c], out_sem.at[p]).wait()
+        take(core_out[p], core_s.at[p])
+        take(cut[p].at[pl.ds(0, RED - 1)], cut_s.at[p])
+        take(mid_in[p].at[pl.ds(0, 7)], mid_s.at[p])
+        take(whole[p].at[pl.ds(0, RED - 1)], who_s.at[p])
     to_sums.wait()
     to_fg.wait()
+    for p in range(PARTS):
+        take(whole[p], oth_s.at[p])
+        keep_own(p).wait()
+        take(kg_hbm[p].at[1 - c], oth_r.at[p])
+
+
+def last_kernel(*refs):
+    kg = refs[:PARTS]
+    fg, sums, kgrad, fg_out, gain_grad, shift_grad, wide, flat, sem = refs[PARTS:]
+    outs = [pltpu.make_async_copy(fg, fg_out, sem.at[9])]
+    outs[0].start()
+    for i, out in ((0, shift_grad), (1, gain_grad)):
+        for half in range(2):
+            flat[i, pl.ds(half * 128, 128)] = sums[2 * i + half]
+        outs.append(pltpu.make_async_copy(flat.at[i], out, sem.at[10 + i]))
+        outs[-1].start()
+    for p in range(PARTS):
+        for k, tap in enumerate(TAPS[p]):
+            at = pl.ds(tap * CH, CH)
+            for half in range(2):
+                v = kg[p][half].astype(F32).reshape(RED * PIECES[p], 128)
+                wide[at, pl.ds(half * 128, 128)] = v[k * CH : (k + 1) * CH]
+            outs.append(pltpu.make_async_copy(wide.at[at], kgrad.at[at], sem.at[tap]))
+            outs[-1].start()
     for out in outs:
         out.wait()
-
-
-def last_kernel(kg, fg_hbm, sums, kgrad, fg_out, gain_grad, shift_grad, sem):
-    copy = pltpu.make_async_copy(fg_hbm, fg_out, sem)
-
-    @pl.when(pl.program_id(0) == 0)
-    def _():
-        copy.start()
-        for half in range(2):
-            at = pl.ds(half * 128, 128)
-            shift_grad[at] = sums[half]
-            gain_grad[at] = sums[2 + half]
-
-    for half in range(2):
-        v = kg[0, half].astype(F32).reshape(RED * PIECE, 128)
-        kgrad[:, pl.ds(half * 128, 128)] = v
-
-    @pl.when(pl.program_id(0) == PARTS - 1)
-    def _():
-        copy.wait()
 
 
 def local(features, cotangent, kernel, norm_gain, norm_shift):
@@ -471,15 +484,17 @@
         pltpu.with_memory_space_constraint(v, pltpu.HBM)
         for v in (features, cotangent, kernel.reshape(9, CH, CH), norm_gain, norm_shift)
     ]
-    fg, kg, sums = pl.pallas_call(
+    rows = [RED * piece for piece in PIECES]
+    shared = [(RED, piece, 128) for piece in PIECES]
+    fg, sums, *kg = pl.pallas_call(
         main_kernel,
-        out_shape=(
+        out_shape=[
             jax.ShapeDtypeStruct((ROWS, COLS, CH), BF16),
-            jax.ShapeDtypeStruct((PARTS, 2, RED, PIECE, 128), BF16),
             jax.ShapeDtypeStruct((4, 128), F32),
-        ),
+        ]
+        + [jax.ShapeDtypeStruct((2,) + shape, BF16) for shape in shared],
         in_specs=[pl.BlockSpec(memory_space=pltpu.HBM)] * 5,
-        out_specs=(any_spec,) * 3,
+        out_specs=[any_spec] * (2 + PARTS),
         scratch_shapes=[
             vmem((ROWS, COLS, CH), BF16),
             vmem((ROWS, COLS, CH), BF16),
@@ -507,18 +522,17 @@
             vmem((4, 128), F32),
             vmem((16, 4, 128), F32),
             vmem((4, 128), F32),
-            vmem((PARTS, RED * PIECE, 128), F32),
-            vmem((PARTS, RED * PIECE, 128), BF16),
-            vmem((PARTS, RED * PIECE, 128), BF16),
-            vmem((PARTS, RED, PIECE, 128), BF16),
-            vmem((PARTS, RED, PIECE, 128), BF16),
-            vmem((PARTS, PIECE, 128), BF16),
-            vmem((PARTS, 8, PIECE, 128), BF16),
-            vmem((PARTS, RED, PIECE, 128), BF16),
-            vmem((PARTS, RED, PIECE, 128), BF16),
+            *[vmem((n, 128), F32) for n in rows],
+            *[vmem((n, 128), BF16) for n in rows],
+            *[vmem((n, 128), BF16) for n in rows],
+            *[vmem(shape, BF16) for shape in shared],
+            *[vmem(shape, BF16) for shape in shared],
+            *[vmem((piece, 128), BF16) for piece in PIECES],
+            *[vmem((8, piece, 128), BF16) for piece in PIECES],
+            *[vmem(shape, BF16) for shape in shared],
             pltpu.SemaphoreType.REGULAR,
             dma((5,)),
-            dma((2 * PARTS + 2,)),
+            dma((PARTS + 2,)),
             dma((2,)), dma((2,)),
             dma((3,)), dma((3,)),
             dma((4,)), dma((4,)),
@@ -533,30 +547,21 @@
         ),
         name="backward",
     )(features, cotangent, kernel, norm_gain, norm_shift)
+    in_vmem = pl.BlockSpec(memory_space=pltpu.VMEM)
     kgrad, fg, gain_grad, shift_grad = pl.pallas_call(
         last_kernel,
-        grid=(PARTS,),
         out_shape=(
             jax.ShapeDtypeStruct((9 * CH, CH), F32),
             jax.ShapeDtypeStruct((ROWS, COLS, CH), BF16),
             jax.ShapeDtypeStruct((CH,), F32),
             jax.ShapeDtypeStruct((CH,), F32),
         ),
-        in_specs=[
-            pl.BlockSpec((1, 2, RED, PIECE, 128), lambda i: (i, 0, 0, 0, 0)),
-            any_spec,
-            pl.BlockSpec((4, 128), lambda i: (0, 0)),
-        ],
-        out_specs=(
-            pl.BlockSpec((RED * PIECE, CH), lambda i: (i, 0)),
-            any_spec,
-            pl.BlockSpec((CH,), lambda i: (0,)),
-            pl.BlockSpec((CH,), lambda i: (0,)),
-        ),
-        scratch_shapes=[dma],
+        in_specs=[in_vmem] * (PARTS + 2),
+        out_specs=(any_spec,) * 4,
+        scratch_shapes=[vmem((9 * CH, CH), F32), vmem((2, CH), F32), dma((12,))],
         compiler_params=pltpu.CompilerParams(vmem_limit_bytes=16 * 2**20),
         name="outputs",
-    )(kg, fg, sums)
+    )(*kg, fg, sums)
     return fg, kgrad.reshape(3, 3, CH, CH), gain_grad, shift_grad
 
 

time: 59.6 us -> 58.9 us (0.988)
  Pallas kernels: 58.8 us -> 58.1 us
    pallas_call x2, Pallas kernels: 58.8 us -> 58.1 us  [the longest x1 56.5 us: local(): pl.pallas_call(main_kernel, out_shape=[jax.ShapeDtypeStruct((ROWS, COLS,...]
where the time goes in v3:
time: 58.9 us; the launch traced here: 58.8 us
  Pallas kernels  58.1 us (99%)
  between operations  0.64 us (1%)
    pallas_call x1, Pallas kernels, local(): pl.pallas_call(main_kernel, out_shape=[jax.ShapeDtypeStruct((ROWS, COLS,...  56.5 us
    pallas_call x1, Pallas kernels, local(): pl.pallas_call(last_kernel, out_shape=(jax.ShapeDtypeStruct((9 * CH, CH),...  1.68 us

profile of v3, /device:TPU:1, one launch (start us, length us, event | category | flops | bytes accessed | tf_op | source)
XLA Modules:
  0.0 58.8 jit_solution(8267128524456374968)
XLA Ops:
  0.6 56.5 %backward.1 = (bf16[128,8,256]{2,1,0:T(8,128)(2,1)S(1)}, f32[4,128]{1,0:T(4,128)S(1)}, bf16[2,32,24,128]{3,2,1,0:T(8,128)(2,1)S(1)}, bf16[2,32,24,128]{3,2,1,0:T(8,128)(2,1)S(1)}, bf16[2,32,24,128]{3,2,1,0:T(8,128)(2,1)S(1)}) custom-call(bf16[128,8,256]{2,1,0:T(8,128)(2,1)} %refs_0_.1, bf16[128,8,256]{2,1,0:T(8,128)(2,1)} %refs_1_.1, ...), custom_call_target="tpu_custom_call" | custom-call | tf_op jit(solution)/shard_map/backward/pallas_call | solution.py:489
  57.1 1.7 %outputs.1 = (f32[2304,256]{1,0:T(8,128)}, bf16[128,8,256]{2,1,0:T(8,128)(2,1)}, f32[256]{0:T(256)}, f32[256]{0:T(256)}) custom-call(bf16[2,32,24,128]{3,2,1,0:T(8,128)(2,1)S(1)} %get-tuple-element.13.refs_0_, bf16[2,32,24,128]{3,2,1,0:T(8,128)(2,1)S(1)} %get-tuple-element.14.refs_1_, bf16[2,32,24,128]{3,2,1,0:T(8,128)(2,1)S(1)} %get-tuple-element.15.refs_2_, ...), custom_call_target="tpu_custom_call" | custom-call | tf_op jit(solution)/shard_map/outputs/pallas_call | solution.py:551

commit v4 on v3

--- a/solution.py
+++ b/solution.py
@@ -414,6 +414,9 @@
     for p in range(PARTS):
         gather(p)
 
+    for p in range(PARTS):
+        hand_over(p)
+
     take(sin2.at[pl.ds(0, 15)], st_r.at[3])
     grads = jnp.sum(sin2[...], axis=0) * (1.0 / ALL_CELLS)
     sumsv[...] = grads
@@ -428,9 +431,6 @@
         fgv[pl.ds(i * 16, 16)] = v.reshape(16, 8, CH).astype(BF16)
     to_fg = pltpu.make_async_copy(fgv, fg_hbm, out_sem.at[PARTS + 1])
     to_fg.start()
-
-    for p in range(PARTS):
-        hand_over(p)
 
     take(edge_out.at[0], edge_s.at[0])
     take(edge_out.at[1], edge_s.at[1])

time: 58.9 us -> 58.9 us (level)
  no operation moved by 1% of the time
where the time goes in v4:
time: 58.9 us; the launch traced here: 58.8 us
  Pallas kernels  58.1 us (99%)
  between operations  0.64 us (1%)
    pallas_call x1, Pallas kernels, local(): pl.pallas_call(main_kernel, out_shape=[jax.ShapeDtypeStruct((ROWS, COLS,...  56.5 us
    pallas_call x1, Pallas kernels, local(): pl.pallas_call(last_kernel, out_shape=(jax.ShapeDtypeStruct((9 * CH, CH),...  1.68 us

profile of v4, /device:TPU:1, one launch (start us, length us, event | category | flops | bytes accessed | tf_op | source)
XLA Modules:
  0.0 58.8 jit_solution(2427556491333744815)
XLA Ops:
  0.6 56.5 %backward.1 = (bf16[128,8,256]{2,1,0:T(8,128)(2,1)S(1)}, f32[4,128]{1,0:T(4,128)S(1)}, bf16[2,32,24,128]{3,2,1,0:T(8,128)(2,1)S(1)}, bf16[2,32,24,128]{3,2,1,0:T(8,128)(2,1)S(1)}, bf16[2,32,24,128]{3,2,1,0:T(8,128)(2,1)S(1)}) custom-call(bf16[128,8,256]{2,1,0:T(8,128)(2,1)} %refs_0_.1, bf16[128,8,256]{2,1,0:T(8,128)(2,1)} %refs_1_.1, ...), custom_call_target="tpu_custom_call" | custom-call | tf_op jit(solution)/shard_map/backward/pallas_call | solution.py:489
  57.1 1.7 %outputs.1 = (f32[2304,256]{1,0:T(8,128)}, bf16[128,8,256]{2,1,0:T(8,128)(2,1)}, f32[256]{0:T(256)}, f32[256]{0:T(256)}) custom-call(bf16[2,32,24,128]{3,2,1,0:T(8,128)(2,1)S(1)} %get-tuple-element.13.refs_0_, bf16[2,32,24,128]{3,2,1,0:T(8,128)(2,1)S(1)} %get-tuple-element.14.refs_1_, bf16[2,32,24,128]{3,2,1,0:T(8,128)(2,1)S(1)} %get-tuple-element.15.refs_2_, ...), custom_call_target="tpu_custom_call" | custom-call | tf_op jit(solution)/shard_map/outputs/pallas_call | solution.py:551
